TPU v7x, 32 devices: a whole 2x2x4 slice. The times are simulated.
32 devices in a mesh: row: 8 (over y, x, core), col: 4 (over z).
Axes of the slice: x: 2, y: 2, z: 4, core: 2. Of those that a mesh axis runs over, the one named last changes fastest.
Arguments:
- object_field: float32 [2, 2, 1024, 512], P(None, None, 'row', 'col'), may hold values from -6 to 6
- probe_field: float32 [2, 128, 128], replicated, may hold values from -6 to 6
- intensity: float32 [8, 4, 6, 128, 128], P('row', 'col'), may hold values from 0.25 to 4
- counts: int32 [8, 4], P('row', 'col'), may hold values from 2 to 6, as said below
- offsets: int32 [8, 4, 6, 2], P('row', 'col'), may hold values from 0 to 64, as said below
Outputs:
- updated_object: float32 [2, 2, 1024, 512], P(None, None, 'row', 'col')
Inputs may be any that keep to these rules, and one draw needn't show every extreme that they name: `counts`: each tile has at least 2 and at most 6 live slots; some tile has exactly 6 and some exactly 2. `offsets`: offsets keep every window inside its bordered tile; both ends of the range occur in every draw.
All inputs are finite; a program needn't handle non-finite values.
Results may differ from a plain program's by a relative error of at most 0.0003.
Values sent between devices are 32-bit elements; how exact they have to be, the bound alone decides.
A program may use at most 64 MiB of HBM per device.

v0:
```python
import functools

import jax
import jax.numpy as jnp
import ml_dtypes
import numpy as np
from jax import lax
from jax.experimental import pallas as pl
from jax.experimental.pallas import tpu as pltpu
from jax.sharding import PartitionSpec as P

BORDER = 32
ITERS = 2
STEP = 0.25
CHIRP = 0.7
DIRS = ((-1, 0), (1, 0), (0, -1), (0, 1), (-1, -1), (-1, 1), (1, -1), (1, 1))
BF = jnp.bfloat16
F32 = jnp.float32
MESH = pl.DeviceIdType.MESH


def tables(n):
    k = np.arange(n)
    ang = -2.0 * np.pi / n * ((k[:, None] * k[None, :]) % n)
    fourier = np.exp(1j * ang) / np.sqrt(n)
    freq = np.where(k < n // 2, k, k - n).astype(np.float64)
    kern = np.exp(-1j * CHIRP * np.pi / n * freq * freq)
    prop = fourier.conj() @ (kern[:, None] * fourier)
    prop = (prop + prop.T) / 2
    left, right = [], []
    for m in (prop, fourier, fourier.conj(), prop.conj()):
        lm = np.block([[m.real, -m.imag], [m.imag, m.real]])
        rm = np.block([[m.real, m.imag], [-m.imag, m.real]])
        for mat, out, axis in ((lm, left, 1), (rm, right, 0)):
            hi = mat.astype(np.float32).astype(ml_dtypes.bfloat16)
            lo = (mat - hi.astype(np.float64)).astype(np.float32).astype(ml_dtypes.bfloat16)
            out.append(np.concatenate([hi, hi, lo], axis=axis))
    return np.stack(left), np.stack(right)


def kernel(nr, nc, obj, probe, inten, counts, offs, lefts, rights, out,
           bord, amp, prop, win2, xc, xr, zb, gpad, acc, core,
           s_ud, s_lr, s_co, r_ud, r_lr, r_co, send_sem, recv_sem):
    n = probe.shape[-1]
    b = BORDER
    slots = inten.shape[0]
    ext = n + 2 * b
    me_r, me_c = lax.axis_index("row"), lax.axis_index("col")
    lane_group = lax.broadcasted_iota(jnp.int32, (1, n), 1) // b

    def exists(dr, dc):
        ok = None
        for pos, step, count in ((me_r, dr, nr), (me_c, dc, nc)):
            if step:
                cond = (pos > 0) if step < 0 else (pos < count - 1)
                ok = cond if ok is None else jnp.logical_and(ok, cond)
        return ok

    def bufs(phase, d):
        if d < 2:
            return s_ud.at[phase, d], r_ud.at[phase, d]
        if d < 4:
            return s_lr.at[phase, d - 2], r_lr.at[phase, d - 2]
        return s_co.at[phase, d - 4], r_co.at[phase, d - 4]

    def message(phase, d):
        src, dst = bufs(phase, d)
        dr, dc = DIRS[d]
        return pltpu.make_async_remote_copy(
            src_ref=src, dst_ref=dst,
            send_sem=send_sem.at[phase, d], recv_sem=recv_sem.at[phase, d],
            device_id=(me_r + dr, me_c + dc), device_id_type=MESH)

    def send(phase):
        for d in (2, 3, 4, 5, 6, 7, 0, 1):
            pl.when(exists(*DIRS[d]))(lambda d=d: message(phase, d).start())

    def wait_recv(phase):
        for d, (dr, dc) in enumerate(DIRS):
            pl.when(exists(-dr, -dc))(lambda d=d: message(phase, d).wait_recv())

    def wait_send(phase):
        for d, (dr, dc) in enumerate(DIRS):
            pl.when(exists(dr, dc))(lambda d=d: message(phase, d).wait_send())

    def pack(take, lane0, row0, rows):
        half = rows // 2
        total = None
        for g in range(4):
            piece = take(g // 2, row0 + (g % 2) * half, half)
            shift = (b * g - lane0) % n
            if shift:
                piece = pltpu.roll(piece, shift, 1)
            total = piece if total is None else jnp.where(lane_group == g, piece, total)
        return total

    def unpack(msg, g, lane0):
        shift = (lane0 - b * g) % n
        return pltpu.roll(msg, shift, 1) if shift else msg

    def pair(left_msg, right_msg, g, left_lane, right_lane):
        zero = jnp.zeros_like(left_msg)
        return jnp.where(lane_group == left_lane // b, unpack(left_msg, g, left_lane),
                         jnp.where(lane_group == right_lane // b,
                                   unpack(right_msg, g, right_lane), zero))

    def send_halo(phase, take):
        for ch in range(2):
            s_ud[phase, 0, ch] = take(ch, 0, b)
            s_ud[phase, 1, ch] = take(ch, n - b, b)
        for i, lane in enumerate((0, n - b)):
            s_lr[phase, i] = pack(take, lane, 0, n)
            s_co[phase, i] = pack(take, lane, 0, b)
            s_co[phase, 2 + i] = pack(take, lane, n - b, b)
        send(phase)

    def recv_halo(phase, sl):
        wait_recv(phase)
        for ch in range(2):
            k = 2 * sl + ch
            bord[k, 0, 0:b] = r_ud[phase, 1, ch]
            bord[k, 0, n + b:ext] = r_ud[phase, 0, ch]
            for h in range(2):
                g = 2 * ch + h
                row = b + h * (n // 2)
                bord[k, 1, row:row + n // 2] = pair(
                    r_lr[phase, 1], r_lr[phase, 0], g, n - b, 0)
                row = h * (b // 2)
                bord[k, 1, row:row + b // 2] = pair(
                    r_co[phase, 3], r_co[phase, 2], g, n - b, 0)
                row = n + b + h * (b // 2)
                bord[k, 1, row:row + b // 2] = pair(
                    r_co[phase, 1], r_co[phase, 0], g, n - b, 0)

    def send_rims(phase, it, sl):
        def take(ch, row, rows):
            return acc[it, sl, ch, 1, row:row + rows]
        for ch in range(2):
            s_ud[phase, 0, ch] = acc[it, sl, ch, 0, 0:b]
            s_ud[phase, 1, ch] = acc[it, sl, ch, 0, n + b:ext]
        for i, lane in enumerate((n - b, 0)):
            s_lr[phase, i] = pack(take, lane, b, n)
            s_co[phase, i] = pack(take, lane, 0, b)
            s_co[phase, 2 + i] = pack(take, lane, n + b, b)
        send(phase)

    def fold(phase, it, sl):
        wait_recv(phase)
        for ch in range(2):
            for h in range(2):
                g = 2 * ch + h
                row = h * (n // 2)
                core[ch, row:row + n // 2] = acc[it, sl, ch, 0, b + row:b + row + n // 2] + pair(
                    r_lr[phase, 1], r_lr[phase, 0], g, 0, n - b)
            core[ch, 0:b] = core[ch, 0:b] + r_ud[phase, 1, ch]
            core[ch, n - b:n] = core[ch, n - b:n] + r_ud[phase, 0, ch]
            for h in range(2):
                g = 2 * ch + h
                row = h * (b // 2)
                core[ch, row:row + b // 2] = core[ch, row:row + b // 2] + pair(
                    r_co[phase, 3], r_co[phase, 2], g, 0, n - b)
                row = n - b + h * (b // 2)
                core[ch, row:row + b // 2] = core[ch, row:row + b // 2] + pair(
                    r_co[phase, 1], r_co[phase, 0], g, 0, n - b)
        for ch in range(2):
            k = 2 * sl + ch
            new = bord[k, 0, b:b + n] - STEP * core[ch]
            if it == ITERS - 1:
                out[sl, ch] = new
            else:
                bord[k, 0, b:b + n] = new

    def parts(x):
        hi = x.astype(BF)
        return hi, (x - hi.astype(F32)).astype(BF)

    def put_col(s, re, im):
        cols = slice(s * n, (s + 1) * n)
        for i, x in enumerate((re, im)):
            hi, lo = parts(x)
            xc[i * n:(i + 1) * n, cols] = hi
            xc[(2 + i) * n:(3 + i) * n, cols] = lo
            xc[(4 + i) * n:(5 + i) * n, cols] = hi

    def transform(t):
        for p in range(slots // 2):
            y = jnp.dot(lefts[t], xc[:, 2 * p * n:2 * (p + 1) * n], preferred_element_type=F32)
            for q in range(2):
                s = 2 * p + q
                rows = slice(s * n, (s + 1) * n)
                for i in range(2):
                    hi, lo = parts(y[i * n:(i + 1) * n, q * n:(q + 1) * n])
                    xr[rows, i * n:(i + 1) * n] = hi
                    xr[rows, (2 + i) * n:(3 + i) * n] = lo
                    xr[rows, (4 + i) * n:(5 + i) * n] = hi
        zb[...] = jnp.dot(xr[...], rights[t], preferred_element_type=F32)

    def result(s):
        return zb[s * n:(s + 1) * n, 0:n], zb[s * n:(s + 1) * n, n:2 * n]

    def window(s, k):
        row, col = offs[0, 0, s, 0], offs[0, 0, s, 1]
        strip = jnp.concatenate([bord[k, h, pl.ds(row, n), :] for h in range(2)], axis=1)
        shift = lax.rem(2 * n + b - col, 2 * n)
        return pltpu.roll(strip, shift, 1)[:, 0:n]

    def place(s, ch, g):
        shift = lax.rem(2 * n - b + offs[0, 0, s, 1], 2 * n)
        wide = jnp.concatenate([g, jnp.zeros_like(g)], axis=1)
        wide = pltpu.roll(wide, shift, 1)
        for h in range(2):
            gpad[s, ch, h, 2 * b:2 * b + n] = wide[:, h * n:(h + 1) * n]

    def gather(it, sl):
        for ch in range(2):
            for h in range(2):
                total = None
                for s in range(slots):
                    term = gpad[s, ch, h, pl.ds(2 * b - offs[0, 0, s, 0], ext), :]
                    total = term if total is None else total + term
                acc[it, sl, ch, h] = total

    for buf in (r_ud, r_lr, r_co):
        buf[...] = jnp.zeros(buf.shape, F32)
    barrier = pltpu.get_barrier_semaphore()
    for dr, dc in DIRS:
        @pl.when(exists(dr, dc))
        def _(dr=dr, dc=dc):
            pl.semaphore_signal(barrier, inc=1, device_id=(me_r + dr, me_c + dc),
                                device_id_type=MESH)
    for s in range(slots):
        amp[s] = jnp.sqrt(inten[s])
        for ch in range(2):
            for h in range(2):
                gpad[s, ch, h, 0:2 * b] = jnp.zeros((2 * b, n), F32)
                gpad[s, ch, h, 2 * b + n:] = jnp.zeros((2 * b, n), F32)
    peers = sum(exists(dr, dc).astype(jnp.int32) for dr, dc in DIRS)
    pl.semaphore_wait(barrier, peers)
    for sl in range(2):
        send_halo(sl, lambda ch, row, rows, sl=sl: obj[sl, ch, row:row + rows, :])
    for sl in range(2):
        for ch in range(2):
            bord[2 * sl + ch, 0, b:b + n] = obj[sl, ch]

    live = counts[0, 0]
    pr, pi = probe.at[0], probe.at[1]
    halo = (0, 1)
    for it in range(ITERS):
        recv_halo(halo[0], 0)
        for s in range(slots):
            ar, ai = window(s, 0), window(s, 1)
            put_col(s, pr[...] * ar - pi[...] * ai, pr[...] * ai + pi[...] * ar)
        transform(0)
        recv_halo(halo[1], 1)
        for s in range(slots):
            ur, ui = result(s)
            ar, ai = window(s, 2), window(s, 3)
            prop[s, 0], prop[s, 1] = ur, ui
            win2[s, 0], win2[s, 1] = ar, ai
            put_col(s, ur * ar - ui * ai, ur * ai + ui * ar)
        transform(1)
        for s in range(slots):
            fr, fi = result(s)
            scale = 1.0 - amp[s] * lax.rsqrt(fr * fr + fi * fi + 1.0)
            scale = scale * (s < live).astype(F32)
            put_col(s, fr * scale, fi * scale)
        transform(2)
        for s in range(slots):
            br, bi = result(s)
            ur, ui = prop[s, 0], prop[s, 1]
            ar, ai = win2[s, 0], win2[s, 1]
            place(s, 0, ur * br + ui * bi)
            place(s, 1, ur * bi - ui * br)
            put_col(s, ar * br + ai * bi, ar * bi - ai * br)
        base = 2 + 4 * it
        gather(it, 1)
        send_rims(base, it, 1)
        transform(3)
        for s in range(slots):
            br, bi = result(s)
            place(s, 0, pr[...] * br + pi[...] * bi)
            place(s, 1, pr[...] * bi - pi[...] * br)
        gather(it, 0)
        send_rims(base + 1, it, 0)
        fold(base, it, 1)
        last = it == ITERS - 1
        if not last:
            send_halo(base + 2, lambda ch, row, rows: bord[2 + ch, 0, b + row:b + row + rows])
        fold(base + 1, it, 0)
        if not last:
            send_halo(base + 3, lambda ch, row, rows: bord[ch, 0, b + row:b + row + rows])
            halo = (base + 3, base + 2)
    for phase in range(4 * ITERS):
        wait_send(phase)


def local(nr, nc, object_field, probe_field, intensity, counts, offsets):
    n = object_field.shape[-1]
    b = BORDER
    slots = intensity.shape[2]
    ext = n + 2 * b
    lefts, rights = tables(n)
    phases = 4 * ITERS
    vmem = pl.BlockSpec(memory_space=pltpu.VMEM)
    smem = pl.BlockSpec(memory_space=pltpu.SMEM)
    messages = [
        pltpu.VMEM((phases, 2, 2, b, n), F32),
        pltpu.VMEM((phases, 2, n // 2, n), F32),
        pltpu.VMEM((phases, 4, b // 2, n), F32),
    ]
    return pl.pallas_call(
        functools.partial(kernel, nr, nc),
        out_shape=jax.ShapeDtypeStruct(object_field.shape, F32),
        in_specs=[vmem, vmem, vmem, smem, smem, vmem, vmem],
        out_specs=vmem,
        scratch_shapes=[
            pltpu.VMEM((4, 2, ext, n), F32),
            pltpu.VMEM((slots, n, n), F32),
            pltpu.VMEM((slots, 2, n, n), F32),
            pltpu.VMEM((slots, 2, n, n), F32),
            pltpu.VMEM((6 * n, slots * n), BF),
            pltpu.VMEM((slots * n, 6 * n), BF),
            pltpu.VMEM((slots * n, 2 * n), F32),
            pltpu.VMEM((slots, 2, 2, n + 4 * b, n), F32),
            pltpu.VMEM((ITERS, 2, 2, 2, ext, n), F32),
            pltpu.VMEM((2, n, n), F32),
            *messages,
            *messages,
            pltpu.SemaphoreType.DMA((phases, 8)),
            pltpu.SemaphoreType.DMA((phases, 8)),
        ],
        compiler_params=pltpu.CompilerParams(
            collective_id=0, has_side_effects=True, vmem_limit_bytes=40 * 1024 * 1024),
    )(object_field, probe_field, intensity[0, 0], counts, offsets,
      jnp.asarray(lefts), jnp.asarray(rights))


def solution(mesh):
    in_specs = (
        P(None, None, "row", "col"),
        P(),
        P("row", "col", None, None, None),
        P("row", "col"),
        P("row", "col", None, None),
    )
    out_specs = P(None, None, "row", "col")
    step = functools.partial(local, mesh.shape["row"], mesh.shape["col"])
    return jax.shard_map(step, mesh=mesh, in_specs=in_specs, out_specs=out_specs, check_vma=False)
```

profile of v0, /device:TPU:1, one launch (start us, length us, event | category | flops | bytes accessed | tf_op | source)
XLA Modules:
  0.0 42.3 jit_solution(17897843619110639011)
XLA Ops:
  0.7 0.8 %copy.8.offs = s32[1,1,6,2]{3,2,1,0:T(8,128)S(1)} copy(s32[1,1,6,2]{2,3,1,0:T(2,128)} %param.11) | data formatting | bytes 96 | tf_op args[4]
  1.4 0.0 copy-start
  1.4 1.4 %copy-done = bf16[4,768,256]{2,1,0:T(8,128)(2,1)S(1)} copy-done((bf16[4,768,256]{2,1,0:T(8,128)(2,1)S(1)}, bf16[4,768,256]{2,1,0:T(8,128)(2,1)}, u32[]{:S(2)}) %copy-start) | copy-done | bytes 1572888
  2.8 0.0 copy-start.1
  2.8 1.4 %copy-done.1 = bf16[4,256,768]{2,1,0:T(8,128)(2,1)S(1)} copy-done((bf16[4,256,768]{2,1,0:T(8,128)(2,1)S(1)}, bf16[4,256,768]{2,1,0:T(8,128)(2,1)}, u32[]{:S(2)}) %copy-start.1) | copy-done | bytes 1572888
  4.2 0.0 copy-start.2
  4.2 1.0 %copy-done.2 = f32[1,1,6,128,128]{4,3,2,1,0:T(8,128)S(1)} copy-done((f32[1,1,6,128,128]{4,3,2,1,0:T(8,128)S(1)}, f32[1,1,6,128,128]{4,3,2,1,0:T(8,128)}, u32[]{:S(2)}) %copy-start.2) | copy-done | bytes 393240
  5.2 0.0 copy-start.3
  5.2 0.9 %copy-done.3 = f32[2,2,128,128]{3,2,1,0:T(8,128)S(1)} copy-done((f32[2,2,128,128]{3,2,1,0:T(8,128)S(1)}, f32[2,2,128,128]{3,2,1,0:T(8,128)}, u32[]{:S(2)}) %copy-start.3) | copy-done | bytes 262168
  6.2 0.0 copy-start.4
  6.2 0.9 %copy-done.4 = f32[2,128,128]{2,1,0:T(8,128)S(1)} copy-done((f32[2,128,128]{2,1,0:T(8,128)S(1)}, f32[2,128,128]{2,1,0:T(8,128)}, u32[]{:S(2)}) %copy-start.4) | copy-done | bytes 131096
  7.1 34.5 %shard_map.73 = f32[2,2,128,128]{3,2,1,0:T(8,128)S(1)} custom-call(f32[2,2,128,128]{3,2,1,0:T(8,128)S(1)} %copy-done.3, f32[2,128,128]{2,1,0:T(8,128)S(1)} %copy-done.4, f32[6,128,128]{2,1,0:T(8,128)S(1)} %bitcast.1, s32[1,1]{1,0:T(1,128)S(6)} %copy.10.counts, s32[1,1,6,2]{3,2,1,0:T(8,128)S(1)} %copy.8.offs, bf16[4,256,768]{2,1,0:T(8,128)(2,1)S(1)} %copy-done.1, ...), custom_call_target="tpu_custom_call" | custom-call | tf_op jit(solution)/shard_map/pallas_call | solution.py:311
  41.6 0.7 %copy.11 = f32[2,2,128,128]{3,2,1,0:T(8,128)} copy(f32[2,2,128,128]{3,2,1,0:T(8,128)S(1)} %shard_map.73) | data formatting | bytes 524288
Async XLA Ops:
  1.4 1.4 %copy-start = (bf16[4,768,256]{2,1,0:T(8,128)(2,1)S(1)}, bf16[4,768,256]{2,1,0:T(8,128)(2,1)}, u32[]{:S(2)}) copy-start(bf16[4,768,256]{2,1,0:T(8,128)(2,1)} %constant.5.clone.rights) | copy-start | bytes 4718596
  2.8 1.4 %copy-start.1 = (bf16[4,256,768]{2,1,0:T(8,128)(2,1)S(1)}, bf16[4,256,768]{2,1,0:T(8,128)(2,1)}, u32[]{:S(2)}) copy-start(bf16[4,256,768]{2,1,0:T(8,128)(2,1)} %constant.4.clone.lefts) | copy-start | bytes 4718596
  4.2 1.0 %copy-start.2 = (f32[1,1,6,128,128]{4,3,2,1,0:T(8,128)S(1)}, f32[1,1,6,128,128]{4,3,2,1,0:T(8,128)}, u32[]{:S(2)}) copy-start(f32[1,1,6,128,128]{4,3,2,1,0:T(8,128)} %param.9) | copy-start | bytes 1179652
  5.2 0.9 %copy-start.3 = (f32[2,2,128,128]{3,2,1,0:T(8,128)S(1)}, f32[2,2,128,128]{3,2,1,0:T(8,128)}, u32[]{:S(2)}) copy-start(f32[2,2,128,128]{3,2,1,0:T(8,128)} %obj.1) | copy-start | bytes 786436
  6.2 0.9 %copy-start.4 = (f32[2,128,128]{2,1,0:T(8,128)S(1)}, f32[2,128,128]{2,1,0:T(8,128)}, u32[]{:S(2)}) copy-start(f32[2,128,128]{2,1,0:T(8,128)} %probe.1) | copy-start | bytes 393220
where the time goes:
time: 42.7 us; the launch traced here: 42.3 us
  Pallas kernels  34.5 us (81%)
  local copies, waits for them, and re-layouts  7.13 us (17%)
  between operations  0.67 us (2%)
    pallas_call x1, Pallas kernels, local(): pl.pallas_call(functools.partial(kernel, nr, nc), out_shape=jax.ShapeDtyp...  34.5 us
    unnamed x12, local copies, waits for them, and re-layouts  7.13 us

commit v1 on v0

--- a/solution.py
+++ b/solution.py
@@ -38,8 +38,8 @@
     return np.stack(left), np.stack(right)
 
 
-def kernel(nr, nc, obj, probe, inten, counts, offs, lefts, rights, out,
-           bord, amp, prop, win2, xc, xr, zb, gpad, acc, core,
+def kernel(nr, nc, obj_h, probe_h, inten_h, counts, offs, lefts_h, rights_h, out,
+           obj, probe, inten, lefts, rights, in_sem, yb, bord, amp, prop, win2, xc, xr, zb, gpad, acc, core,
            s_ud, s_lr, s_co, r_ud, r_lr, r_co, send_sem, recv_sem):
     n = probe.shape[-1]
     b = BORDER
@@ -182,58 +182,76 @@
             xc[(2 + i) * n:(3 + i) * n, cols] = lo
             xc[(4 + i) * n:(5 + i) * n, cols] = hi
 
-    def transform(t):
-        for p in range(slots // 2):
-            y = jnp.dot(lefts[t], xc[:, 2 * p * n:2 * (p + 1) * n], preferred_element_type=F32)
-            for q in range(2):
-                s = 2 * p + q
-                rows = slice(s * n, (s + 1) * n)
-                for i in range(2):
-                    hi, lo = parts(y[i * n:(i + 1) * n, q * n:(q + 1) * n])
-                    xr[rows, i * n:(i + 1) * n] = hi
-                    xr[rows, (2 + i) * n:(3 + i) * n] = lo
-                    xr[rows, (4 + i) * n:(5 + i) * n] = hi
-        zb[...] = jnp.dot(xr[...], rights[t], preferred_element_type=F32)
+    def left(t, p):
+        cols = slice(2 * p * n, 2 * (p + 1) * n)
+        yb[:, cols] = jnp.dot(lefts[t], xc[:, cols], preferred_element_type=F32)
+
+    def right(t, p):
+        for s in (2 * p, 2 * p + 1):
+            rows = slice(s * n, (s + 1) * n)
+            for i in range(2):
+                hi, lo = parts(yb[i * n:(i + 1) * n, rows])
+                xr[rows, i * n:(i + 1) * n] = hi
+                xr[rows, (2 + i) * n:(3 + i) * n] = lo
+                xr[rows, (4 + i) * n:(5 + i) * n] = hi
+        rows = slice(2 * p * n, 2 * (p + 1) * n)
+        zb[rows] = jnp.dot(xr[rows], rights[t], preferred_element_type=F32)
 
     def result(s):
         return zb[s * n:(s + 1) * n, 0:n], zb[s * n:(s + 1) * n, n:2 * n]
 
     def window(s, k):
-        row, col = offs[0, 0, s, 0], offs[0, 0, s, 1]
+        row, col = offs[0, s], offs[1, s]
         strip = jnp.concatenate([bord[k, h, pl.ds(row, n), :] for h in range(2)], axis=1)
         shift = lax.rem(2 * n + b - col, 2 * n)
         return pltpu.roll(strip, shift, 1)[:, 0:n]
 
     def place(s, ch, g):
-        shift = lax.rem(2 * n - b + offs[0, 0, s, 1], 2 * n)
+        shift = lax.rem(2 * n - b + offs[1, s], 2 * n)
         wide = jnp.concatenate([g, jnp.zeros_like(g)], axis=1)
         wide = pltpu.roll(wide, shift, 1)
         for h in range(2):
             gpad[s, ch, h, 2 * b:2 * b + n] = wide[:, h * n:(h + 1) * n]
 
-    def gather(it, sl):
-        for ch in range(2):
-            for h in range(2):
+    def gather(it, sl, ranges):
+        for ch in range(2):
+            for h, row, rows in ranges:
                 total = None
                 for s in range(slots):
-                    term = gpad[s, ch, h, pl.ds(2 * b - offs[0, 0, s, 0], ext), :]
+                    start = 2 * b + row - offs[0, s]
+                    term = gpad[s, ch, h, pl.ds(start, rows), :]
                     total = term if total is None else total + term
-                acc[it, sl, ch, h] = total
-
-    for buf in (r_ud, r_lr, r_co):
-        buf[...] = jnp.zeros(buf.shape, F32)
+                acc[it, sl, ch, h, row:row + rows] = total
+
+    rims = ((1, 0, ext), (0, 0, b), (0, n + b, b))
+    middle = ((0, b, n),)
+
+    def fetch(i):
+        pairs = ((obj_h, obj), (probe_h, probe), (lefts_h.at[0], lefts.at[0]),
+                 (rights_h.at[0], rights.at[0]), (inten_h.at[0, 0], inten),
+                 (lefts_h.at[1:], lefts.at[1:]), (rights_h.at[1:], rights.at[1:]))
+        return pltpu.make_async_copy(*pairs[i], in_sem.at[i])
+
+    for i in range(7):
+        fetch(i).start()
     barrier = pltpu.get_barrier_semaphore()
     for dr, dc in DIRS:
         @pl.when(exists(dr, dc))
         def _(dr=dr, dc=dc):
             pl.semaphore_signal(barrier, inc=1, device_id=(me_r + dr, me_c + dc),
                                 device_id_type=MESH)
+    for d, (dr, dc) in enumerate(DIRS):
+        @pl.when(jnp.logical_not(exists(-dr, -dc)))
+        def _(d=d):
+            for phase in range(4 * ITERS):
+                dst = bufs(phase, d)[1]
+                dst[...] = jnp.zeros(dst.shape, F32)
     for s in range(slots):
-        amp[s] = jnp.sqrt(inten[s])
         for ch in range(2):
             for h in range(2):
                 gpad[s, ch, h, 0:2 * b] = jnp.zeros((2 * b, n), F32)
                 gpad[s, ch, h, 2 * b + n:] = jnp.zeros((2 * b, n), F32)
+    fetch(0).wait()
     peers = sum(exists(dr, dc).astype(jnp.int32) for dr, dc in DIRS)
     pl.semaphore_wait(barrier, peers)
     for sl in range(2):
@@ -241,55 +259,105 @@
     for sl in range(2):
         for ch in range(2):
             bord[2 * sl + ch, 0, b:b + n] = obj[sl, ch]
+    for i in range(1, 5):
+        fetch(i).wait()
+    for s in range(slots):
+        amp[s] = jnp.sqrt(inten[s])
 
     live = counts[0, 0]
     pr, pi = probe.at[0], probe.at[1]
-    halo = (0, 1)
+
+    def both(step):
+        def run(p):
+            for s in (2 * p, 2 * p + 1):
+                step(s)
+        return run
+
+    def incident(s):
+        ar, ai = window(s, 0), window(s, 1)
+        put_col(s, pr[...] * ar - pi[...] * ai, pr[...] * ai + pi[...] * ar)
+
+    def second_windows():
+        for s in range(slots):
+            win2[s, 0], win2[s, 1] = window(s, 2), window(s, 3)
+
+    def exit_wave(s):
+        ur, ui = result(s)
+        ar, ai = win2[s, 0], win2[s, 1]
+        prop[s, 0], prop[s, 1] = ur, ui
+        put_col(s, ur * ar - ui * ai, ur * ai + ui * ar)
+
+    def residual(s):
+        fr, fi = result(s)
+        scale = 1.0 - amp[s] * lax.rsqrt(fr * fr + fi * fi + 1.0)
+        scale = scale * (s < live).astype(F32)
+        put_col(s, fr * scale, fi * scale)
+
+    def back_wave(s):
+        br, bi = result(s)
+        ar, ai = win2[s, 0], win2[s, 1]
+        put_col(s, ar * br + ai * bi, ar * bi - ai * br)
+
+    def grad_second(s):
+        br, bi = result(s)
+        ur, ui = prop[s, 0], prop[s, 1]
+        place(s, 0, ur * br + ui * bi)
+        place(s, 1, ur * bi - ui * br)
+
+    def grad_first(s):
+        br, bi = result(s)
+        place(s, 0, pr[...] * br + pi[...] * bi)
+        place(s, 1, pr[...] * bi - pi[...] * br)
+
+    def prepare_and_left(prep, t):
+        for p in range(slots // 2):
+            both(prep)(p)
+            left(t, p)
+
+    def all_right(t):
+        for p in range(slots // 2):
+            right(t, p)
+
     for it in range(ITERS):
-        recv_halo(halo[0], 0)
-        for s in range(slots):
-            ar, ai = window(s, 0), window(s, 1)
-            put_col(s, pr[...] * ar - pi[...] * ai, pr[...] * ai + pi[...] * ar)
-        transform(0)
-        recv_halo(halo[1], 1)
-        for s in range(slots):
-            ur, ui = result(s)
-            ar, ai = window(s, 2), window(s, 3)
-            prop[s, 0], prop[s, 1] = ur, ui
-            win2[s, 0], win2[s, 1] = ar, ai
-            put_col(s, ur * ar - ui * ai, ur * ai + ui * ar)
-        transform(1)
-        for s in range(slots):
-            fr, fi = result(s)
-            scale = 1.0 - amp[s] * lax.rsqrt(fr * fr + fi * fi + 1.0)
-            scale = scale * (s < live).astype(F32)
-            put_col(s, fr * scale, fi * scale)
-        transform(2)
-        for s in range(slots):
-            br, bi = result(s)
-            ur, ui = prop[s, 0], prop[s, 1]
-            ar, ai = win2[s, 0], win2[s, 1]
-            place(s, 0, ur * br + ui * bi)
-            place(s, 1, ur * bi - ui * br)
-            put_col(s, ar * br + ai * bi, ar * bi - ai * br)
         base = 2 + 4 * it
-        gather(it, 1)
+        last = it == ITERS - 1
+        if it:
+            recv_halo(base - 2, 1)
+            second_windows()
+            recv_halo(base - 1, 0)
+        else:
+            recv_halo(0, 0)
+        prepare_and_left(incident, 0)
+        if not it:
+            recv_halo(1, 1)
+            second_windows()
+        all_right(0)
+        if not it:
+            for i in (5, 6):
+                fetch(i).wait()
+        prepare_and_left(exit_wave, 1)
+        all_right(1)
+        prepare_and_left(residual, 2)
+        all_right(2)
+        for p in range(slots // 2):
+            both(back_wave)(p)
+            left(3, p)
+            both(grad_second)(p)
+        gather(it, 1, rims)
         send_rims(base, it, 1)
-        transform(3)
-        for s in range(slots):
-            br, bi = result(s)
-            place(s, 0, pr[...] * br + pi[...] * bi)
-            place(s, 1, pr[...] * bi - pi[...] * br)
-        gather(it, 0)
+        gather(it, 1, middle)
+        all_right(3)
+        for p in range(slots // 2):
+            both(grad_first)(p)
+        gather(it, 0, rims)
         send_rims(base + 1, it, 0)
+        gather(it, 0, middle)
         fold(base, it, 1)
-        last = it == ITERS - 1
         if not last:
             send_halo(base + 2, lambda ch, row, rows: bord[2 + ch, 0, b + row:b + row + rows])
         fold(base + 1, it, 0)
         if not last:
             send_halo(base + 3, lambda ch, row, rows: bord[ch, 0, b + row:b + row + rows])
-            halo = (base + 3, base + 2)
     for phase in range(4 * ITERS):
         wait_send(phase)
 
@@ -302,6 +370,7 @@
     lefts, rights = tables(n)
     phases = 4 * ITERS
     vmem = pl.BlockSpec(memory_space=pltpu.VMEM)
+    hbm = pl.BlockSpec(memory_space=pltpu.HBM)
     smem = pl.BlockSpec(memory_space=pltpu.SMEM)
     messages = [
         pltpu.VMEM((phases, 2, 2, b, n), F32),
@@ -311,9 +380,16 @@
     return pl.pallas_call(
         functools.partial(kernel, nr, nc),
         out_shape=jax.ShapeDtypeStruct(object_field.shape, F32),
-        in_specs=[vmem, vmem, vmem, smem, smem, vmem, vmem],
+        in_specs=[hbm, hbm, hbm, smem, smem, hbm, hbm],
         out_specs=vmem,
         scratch_shapes=[
+            pltpu.VMEM(object_field.shape, F32),
+            pltpu.VMEM(probe_field.shape, F32),
+            pltpu.VMEM((slots, n, n), F32),
+            pltpu.VMEM(lefts.shape, BF),
+            pltpu.VMEM(rights.shape, BF),
+            pltpu.SemaphoreType.DMA((7,)),
+            pltpu.VMEM((2 * n, slots * n), F32),
             pltpu.VMEM((4, 2, ext, n), F32),
             pltpu.VMEM((slots, n, n), F32),
             pltpu.VMEM((slots, 2, n, n), F32),
@@ -330,8 +406,8 @@
             pltpu.SemaphoreType.DMA((phases, 8)),
         ],
         compiler_params=pltpu.CompilerParams(
-            collective_id=0, has_side_effects=True, vmem_limit_bytes=40 * 1024 * 1024),
-    )(object_field, probe_field, intensity[0, 0], counts, offsets,
+            collective_id=0, has_side_effects=True, vmem_limit_bytes=63 * 1024 * 1024),
+    )(object_field, probe_field, intensity, counts, jnp.swapaxes(offsets[0, 0], 0, 1),
       jnp.asarray(lefts), jnp.asarray(rights))
 
 

time: 42.7 us -> 34.5 us (0.81)
  local copies, waits for them, and re-layouts: 7.13 us -> 1.67 us
  Pallas kernels: 34.5 us -> 32 us
    unnamed x12 -> x1, local copies, waits for them, and re-layouts: 7.13 us -> 1.67 us
    pallas_call x1, Pallas kernels: 34.5 us -> 32 us  [local(): pl.pallas_call(functools.partial(kernel, nr, nc), out_shape=jax.ShapeDtyp...]
where the time goes in v1:
time: 34.5 us; the launch traced here: 34.4 us
  Pallas kernels  32 us (93%)
  local copies, waits for them, and re-layouts  1.67 us (5%)
  between operations  0.66 us (2%)
    pallas_call x1, Pallas kernels, local(): pl.pallas_call(functools.partial(kernel, nr, nc), out_shape=jax.ShapeDtyp...  32 us
    unnamed x1, local copies, waits for them, and re-layouts  1.67 us

profile of v1, /device:TPU:1, one launch (start us, length us, event | category | flops | bytes accessed | tf_op | source)
XLA Modules:
  0.0 34.4 jit_solution(6951844771376583654)
XLA Ops:
  0.7 32.0 %shard_map.73 = f32[2,2,128,128]{3,2,1,0:T(8,128)} custom-call(f32[2,2,128,128]{3,2,1,0:T(8,128)} %obj_h.1, f32[2,128,128]{2,1,0:T(8,128)} %probe_h.1, f32[1,1,6,128,128]{4,3,2,1,0:T(8,128)} %inten_h.1, s32[1,1]{1,0:T(1,128)S(6)} %copy.9.counts, s32[2,6]{1,0:T(2,128)} %bitcast.3, bf16[4,256,768]{2,1,0:T(8,128)(2,1)} %constant.4.clone.lefts_h, ...), custom_call_target="tpu_custom_call" | custom-call | tf_op jit(solution)/shard_map/pallas_call | solution.py:380
  32.7 1.7 %copy.10 = f32[2,2,128,128]{3,2,1,0:T(8,128)} copy(f32[2,2,128,128]{3,2,1,0:T(8,128)} %shard_map.73) | data formatting | bytes 524288

commit v2 on v1

--- a/solution.py
+++ b/solution.py
@@ -27,19 +27,21 @@
     kern = np.exp(-1j * CHIRP * np.pi / n * freq * freq)
     prop = fourier.conj() @ (kern[:, None] * fourier)
     prop = (prop + prop.T) / 2
-    left, right = [], []
-    for m in (prop, fourier, fourier.conj(), prop.conj()):
-        lm = np.block([[m.real, -m.imag], [m.imag, m.real]])
-        rm = np.block([[m.real, m.imag], [-m.imag, m.real]])
-        for mat, out, axis in ((lm, left, 1), (rm, right, 0)):
+    out = []
+    for m in (prop, fourier):
+        for mat in (np.block([[m.real, -m.imag], [m.imag, m.real]]),
+                    np.block([[m.real, m.imag], [-m.imag, m.real]])):
             hi = mat.astype(np.float32).astype(ml_dtypes.bfloat16)
             lo = (mat - hi.astype(np.float64)).astype(np.float32).astype(ml_dtypes.bfloat16)
-            out.append(np.concatenate([hi, hi, lo], axis=axis))
-    return np.stack(left), np.stack(right)
-
-
-def kernel(nr, nc, obj_h, probe_h, inten_h, counts, offs, lefts_h, rights_h, out,
-           obj, probe, inten, lefts, rights, in_sem, yb, bord, amp, prop, win2, xc, xr, zb, gpad, acc, core,
+            out.append(np.stack([hi, lo]))
+    return np.stack(out)
+
+
+FACTORS = ((0, 1), (2, 3), (3, 2), (1, 0))
+
+
+def kernel(nr, nc, obj_h, probe_h, inten_h, counts, offs, tabs_h, out,
+           obj, probe, inten, tabs, in_sem, yb, bord, amp, prop, win2, xc, xr, zb, gpad, acc, core,
            s_ud, s_lr, s_co, r_ud, r_lr, r_co, send_sem, recv_sem):
     n = probe.shape[-1]
     b = BORDER
@@ -180,11 +182,14 @@
             hi, lo = parts(x)
             xc[i * n:(i + 1) * n, cols] = hi
             xc[(2 + i) * n:(3 + i) * n, cols] = lo
-            xc[(4 + i) * n:(5 + i) * n, cols] = hi
+
+    dot = functools.partial(jnp.dot, preferred_element_type=F32)
 
     def left(t, p):
         cols = slice(2 * p * n, 2 * (p + 1) * n)
-        yb[:, cols] = jnp.dot(lefts[t], xc[:, cols], preferred_element_type=F32)
+        hi, lo = xc[0:2 * n, cols], xc[2 * n:4 * n, cols]
+        m = FACTORS[t][0]
+        yb[:, cols] = dot(tabs[m, 0], hi) + (dot(tabs[m, 0], lo) + dot(tabs[m, 1], hi))
 
     def right(t, p):
         for s in (2 * p, 2 * p + 1):
@@ -193,9 +198,10 @@
                 hi, lo = parts(yb[i * n:(i + 1) * n, rows])
                 xr[rows, i * n:(i + 1) * n] = hi
                 xr[rows, (2 + i) * n:(3 + i) * n] = lo
-                xr[rows, (4 + i) * n:(5 + i) * n] = hi
         rows = slice(2 * p * n, 2 * (p + 1) * n)
-        zb[rows] = jnp.dot(xr[rows], rights[t], preferred_element_type=F32)
+        hi, lo = xr[rows, 0:2 * n], xr[rows, 2 * n:4 * n]
+        m = FACTORS[t][1]
+        zb[rows] = dot(hi, tabs[m, 0]) + (dot(lo, tabs[m, 0]) + dot(hi, tabs[m, 1]))
 
     def result(s):
         return zb[s * n:(s + 1) * n, 0:n], zb[s * n:(s + 1) * n, n:2 * n]
@@ -227,12 +233,10 @@
     middle = ((0, b, n),)
 
     def fetch(i):
-        pairs = ((obj_h, obj), (probe_h, probe), (lefts_h.at[0], lefts.at[0]),
-                 (rights_h.at[0], rights.at[0]), (inten_h.at[0, 0], inten),
-                 (lefts_h.at[1:], lefts.at[1:]), (rights_h.at[1:], rights.at[1:]))
+        pairs = ((obj_h, obj), (probe_h, probe), (tabs_h, tabs), (inten_h.at[0, 0], inten))
         return pltpu.make_async_copy(*pairs[i], in_sem.at[i])
 
-    for i in range(7):
+    for i in range(4):
         fetch(i).start()
     barrier = pltpu.get_barrier_semaphore()
     for dr, dc in DIRS:
@@ -259,7 +263,7 @@
     for sl in range(2):
         for ch in range(2):
             bord[2 * sl + ch, 0, b:b + n] = obj[sl, ch]
-    for i in range(1, 5):
+    for i in range(1, 4):
         fetch(i).wait()
     for s in range(slots):
         amp[s] = jnp.sqrt(inten[s])
@@ -332,9 +336,6 @@
             recv_halo(1, 1)
             second_windows()
         all_right(0)
-        if not it:
-            for i in (5, 6):
-                fetch(i).wait()
         prepare_and_left(exit_wave, 1)
         all_right(1)
         prepare_and_left(residual, 2)
@@ -367,7 +368,7 @@
     b = BORDER
     slots = intensity.shape[2]
     ext = n + 2 * b
-    lefts, rights = tables(n)
+    tabs = tables(n)
     phases = 4 * ITERS
     vmem = pl.BlockSpec(memory_space=pltpu.VMEM)
     hbm = pl.BlockSpec(memory_space=pltpu.HBM)
@@ -380,22 +381,21 @@
     return pl.pallas_call(
         functools.partial(kernel, nr, nc),
         out_shape=jax.ShapeDtypeStruct(object_field.shape, F32),
-        in_specs=[hbm, hbm, hbm, smem, smem, hbm, hbm],
+        in_specs=[hbm, hbm, hbm, smem, smem, hbm],
         out_specs=vmem,
         scratch_shapes=[
             pltpu.VMEM(object_field.shape, F32),
             pltpu.VMEM(probe_field.shape, F32),
             pltpu.VMEM((slots, n, n), F32),
-            pltpu.VMEM(lefts.shape, BF),
-            pltpu.VMEM(rights.shape, BF),
-            pltpu.SemaphoreType.DMA((7,)),
+            pltpu.VMEM(tabs.shape, BF),
+            pltpu.SemaphoreType.DMA((4,)),
             pltpu.VMEM((2 * n, slots * n), F32),
             pltpu.VMEM((4, 2, ext, n), F32),
             pltpu.VMEM((slots, n, n), F32),
             pltpu.VMEM((slots, 2, n, n), F32),
             pltpu.VMEM((slots, 2, n, n), F32),
-            pltpu.VMEM((6 * n, slots * n), BF),
-            pltpu.VMEM((slots * n, 6 * n), BF),
+            pltpu.VMEM((4 * n, slots * n), BF),
+            pltpu.VMEM((slots * n, 4 * n), BF),
             pltpu.VMEM((slots * n, 2 * n), F32),
             pltpu.VMEM((slots, 2, 2, n + 4 * b, n), F32),
             pltpu.VMEM((ITERS, 2, 2, 2, ext, n), F32),
@@ -408,7 +408,7 @@
         compiler_params=pltpu.CompilerParams(
             collective_id=0, has_side_effects=True, vmem_limit_bytes=63 * 1024 * 1024),
     )(object_field, probe_field, intensity, counts, jnp.swapaxes(offsets[0, 0], 0, 1),
-      jnp.asarray(lefts), jnp.asarray(rights))
+      jnp.asarray(tabs))
 
 
 def solution(mesh):

time: 34.5 us -> 34.1 us (0.988)
    pallas_call x1, Pallas kernels: 32 us -> 31.7 us  [local(): pl.pallas_call(functools.partial(kernel, nr, nc), out_shape=jax.ShapeDtyp...]
where the time goes in v2:
time: 34.1 us; the launch traced here: 34 us
  Pallas kernels  31.7 us (93%)
  local copies, waits for them, and re-layouts  1.67 us (5%)
  between operations  0.66 us (2%)
    pallas_call x1, Pallas kernels, local(): pl.pallas_call(functools.partial(kernel, nr, nc), out_shape=jax.ShapeDtyp...  31.7 us
    unnamed x1, local copies, waits for them, and re-layouts  1.67 us

profile of v2, /device:TPU:1, one launch (start us, length us, event | category | flops | bytes accessed | tf_op | source)
XLA Modules:
  0.0 34.0 jit_solution(4098662473030309712)
XLA Ops:
  0.7 31.7 %shard_map.64 = f32[2,2,128,128]{3,2,1,0:T(8,128)} custom-call(f32[2,2,128,128]{3,2,1,0:T(8,128)} %obj_h.1, f32[2,128,128]{2,1,0:T(8,128)} %probe_h.1, f32[1,1,6,128,128]{4,3,2,1,0:T(8,128)} %inten_h.1, s32[1,1]{1,0:T(1,128)S(6)} %copy.8.counts, s32[2,6]{1,0:T(2,128)} %bitcast.3, bf16[4,2,256,256]{3,2,1,0:T(8,128)(2,1)} %constant.2.clone.tabs_h), custom_call_target="tpu_custom_call" | custom-call | tf_op jit(solution)/shard_map/pallas_call | solution.py:381
  32.3 1.7 %copy.9 = f32[2,2,128,128]{3,2,1,0:T(8,128)} copy(f32[2,2,128,128]{3,2,1,0:T(8,128)} %shard_map.64) | data formatting | bytes 524288

commit v3 on v2

--- a/solution.py
+++ b/solution.py
@@ -41,14 +41,15 @@
 
 
 def kernel(nr, nc, obj_h, probe_h, inten_h, counts, offs, tabs_h, out,
-           obj, probe, inten, tabs, in_sem, yb, bord, amp, prop, win2, xc, xr, zb, gpad, acc, core,
+           obj, probe, inten, tabs, in_sem, bord, amp, prop, win2, xc, xr, zb, gpad, acc, core,
            s_ud, s_lr, s_co, r_ud, r_lr, r_co, send_sem, recv_sem):
     n = probe.shape[-1]
     b = BORDER
     slots = inten.shape[0]
     ext = n + 2 * b
     me_r, me_c = lax.axis_index("row"), lax.axis_index("col")
-    lane_group = lax.broadcasted_iota(jnp.int32, (1, n), 1) // b
+    lane = lax.broadcasted_iota(jnp.int32, (1, n), 1)
+    lane_group = lane // b
 
     def exists(dr, dc):
         ok = None
@@ -189,15 +190,15 @@
         cols = slice(2 * p * n, 2 * (p + 1) * n)
         hi, lo = xc[0:2 * n, cols], xc[2 * n:4 * n, cols]
         m = FACTORS[t][0]
-        yb[:, cols] = dot(tabs[m, 0], hi) + (dot(tabs[m, 0], lo) + dot(tabs[m, 1], hi))
-
-    def right(t, p):
-        for s in (2 * p, 2 * p + 1):
-            rows = slice(s * n, (s + 1) * n)
+        y = dot(tabs[m, 0], hi) + (dot(tabs[m, 0], lo) + dot(tabs[m, 1], hi))
+        for q in range(2):
+            rows = slice((2 * p + q) * n, (2 * p + q + 1) * n)
             for i in range(2):
-                hi, lo = parts(yb[i * n:(i + 1) * n, rows])
+                hi, lo = parts(y[i * n:(i + 1) * n, q * n:(q + 1) * n])
                 xr[rows, i * n:(i + 1) * n] = hi
                 xr[rows, (2 + i) * n:(3 + i) * n] = lo
+
+    def right(t, p):
         rows = slice(2 * p * n, 2 * (p + 1) * n)
         hi, lo = xr[rows, 0:2 * n], xr[rows, 2 * n:4 * n]
         m = FACTORS[t][1]
@@ -208,16 +209,18 @@
 
     def window(s, k):
         row, col = offs[0, s], offs[1, s]
-        strip = jnp.concatenate([bord[k, h, pl.ds(row, n), :] for h in range(2)], axis=1)
-        shift = lax.rem(2 * n + b - col, 2 * n)
-        return pltpu.roll(strip, shift, 1)[:, 0:n]
+        shift = lax.rem(n + b - col, n)
+        near, far = [pltpu.roll(bord[k, h, pl.ds(row, n), :], shift, 1) for h in range(2)]
+        pos = lane + (col - b)
+        return jnp.where((pos >= 0) & (pos < n), near, far)
 
     def place(s, ch, g):
-        shift = lax.rem(2 * n - b + offs[1, s], 2 * n)
-        wide = jnp.concatenate([g, jnp.zeros_like(g)], axis=1)
-        wide = pltpu.roll(wide, shift, 1)
-        for h in range(2):
-            gpad[s, ch, h, 2 * b:2 * b + n] = wide[:, h * n:(h + 1) * n]
+        col = offs[1, s]
+        turned = pltpu.roll(g, lax.rem(n + col - b, n), 1)
+        pos = lane - (col - b)
+        near = (pos >= 0) & (pos < n)
+        gpad[s, ch, 0, 2 * b:2 * b + n] = jnp.where(near, turned, 0.0)
+        gpad[s, ch, 1, 2 * b:2 * b + n] = jnp.where(near, 0.0, turned)
 
     def gather(it, sl, ranges):
         for ch in range(2):
@@ -363,6 +366,15 @@
         wait_send(phase)
 
 
+def move(src, dst, sem):
+    pieces = [(i, j) for i in range(src.shape[0]) for j in range(src.shape[1])]
+    copies = [pltpu.make_async_copy(src.at[i, j], dst.at[i, j], sem.at[i, j]) for i, j in pieces]
+    for copy in copies:
+        copy.start()
+    for copy in copies:
+        copy.wait()
+
+
 def local(nr, nc, object_field, probe_field, intensity, counts, offsets):
     n = object_field.shape[-1]
     b = BORDER
@@ -378,7 +390,7 @@
         pltpu.VMEM((phases, 2, n // 2, n), F32),
         pltpu.VMEM((phases, 4, b // 2, n), F32),
     ]
-    return pl.pallas_call(
+    updated = pl.pallas_call(
         functools.partial(kernel, nr, nc),
         out_shape=jax.ShapeDtypeStruct(object_field.shape, F32),
         in_specs=[hbm, hbm, hbm, smem, smem, hbm],
@@ -389,7 +401,6 @@
             pltpu.VMEM((slots, n, n), F32),
             pltpu.VMEM(tabs.shape, BF),
             pltpu.SemaphoreType.DMA((4,)),
-            pltpu.VMEM((2 * n, slots * n), F32),
             pltpu.VMEM((4, 2, ext, n), F32),
             pltpu.VMEM((slots, n, n), F32),
             pltpu.VMEM((slots, 2, n, n), F32),
@@ -409,6 +420,14 @@
             collective_id=0, has_side_effects=True, vmem_limit_bytes=63 * 1024 * 1024),
     )(object_field, probe_field, intensity, counts, jnp.swapaxes(offsets[0, 0], 0, 1),
       jnp.asarray(tabs))
+    return pl.pallas_call(
+        move,
+        out_shape=jax.ShapeDtypeStruct(updated.shape, F32),
+        in_specs=[hbm],
+        out_specs=hbm,
+        scratch_shapes=[pltpu.SemaphoreType.DMA(updated.shape[:2])],
+        compiler_params=pltpu.CompilerParams(vmem_limit_bytes=63 * 1024 * 1024),
+    )(updated)
 
 
 def solution(mesh):

time: 34.1 us -> 41.4 us (1.21)
  Pallas kernels: 31.7 us -> 40.5 us
  local copies, waits for them, and re-layouts: 1.67 us -> 0 us
    pallas_call x0 -> x1, Pallas kernels: none -> 9.08 us  [local(): pl.pallas_call(move, out_shape=jax.ShapeDtypeStruct(updated.shape, F32),...]
    unnamed x1 -> x0, local copies, waits for them, and re-layouts: 1.67 us -> none
where the time goes in v3:
time: 41.4 us; the launch traced here: 41.2 us
  Pallas kernels  40.5 us (98%)
  between operations  0.66 us (2%)
    pallas_call x1, Pallas kernels, local(): pl.pallas_call(functools.partial(kernel, nr, nc), out_shape=jax.ShapeDtyp...  31.5 us
    pallas_call x1, Pallas kernels, local(): pl.pallas_call(move, out_shape=jax.ShapeDtypeStruct(updated.shape, F32),...  9.08 us

profile of v3, /device:TPU:1, one launch (start us, length us, event | category | flops | bytes accessed | tf_op | source)
XLA Modules:
  0.0 41.2 jit_solution(6359660092592572054)
XLA Ops:
  0.7 31.5 %shard_map.64.src = f32[2,2,128,128]{3,2,1,0:T(8,128)} custom-call(f32[2,2,128,128]{3,2,1,0:T(8,128)} %obj_h.1, f32[2,128,128]{2,1,0:T(8,128)} %probe_h.1, f32[1,1,6,128,128]{4,3,2,1,0:T(8,128)} %inten_h.1, s32[1,1]{1,0:T(1,128)S(6)} %copy.7.counts, s32[2,6]{1,0:T(2,128)} %bitcast.3, bf16[4,2,256,256]{3,2,1,0:T(8,128)(2,1)} %constant.2.clone.tabs_h), custom_call_target="tpu_custom_call" | custom-call | tf_op jit(solution)/shard_map/pallas_call | solution.py:393
  32.1 9.1 %shard_map.65 = f32[2,2,128,128]{3,2,1,0:T(8,128)} custom-call(f32[2,2,128,128]{3,2,1,0:T(8,128)} %shard_map.64.src), custom_call_target="tpu_custom_call" | custom-call | tf_op jit(solution)/shard_map/pallas_call | solution.py:423

commit v4 on v3

--- a/solution.py
+++ b/solution.py
@@ -190,7 +190,8 @@
         cols = slice(2 * p * n, 2 * (p + 1) * n)
         hi, lo = xc[0:2 * n, cols], xc[2 * n:4 * n, cols]
         m = FACTORS[t][0]
-        y = dot(tabs[m, 0], hi) + (dot(tabs[m, 0], lo) + dot(tabs[m, 1], hi))
+        y = dot(jnp.concatenate([tabs[m, 0], tabs[m, 0], tabs[m, 1]], axis=1),
+                jnp.concatenate([hi, lo, hi], axis=0))
         for q in range(2):
             rows = slice((2 * p + q) * n, (2 * p + q + 1) * n)
             for i in range(2):
@@ -202,7 +203,8 @@
         rows = slice(2 * p * n, 2 * (p + 1) * n)
         hi, lo = xr[rows, 0:2 * n], xr[rows, 2 * n:4 * n]
         m = FACTORS[t][1]
-        zb[rows] = dot(hi, tabs[m, 0]) + (dot(lo, tabs[m, 0]) + dot(hi, tabs[m, 1]))
+        zb[rows] = dot(jnp.concatenate([hi, lo, hi], axis=1),
+                       jnp.concatenate([tabs[m, 0], tabs[m, 0], tabs[m, 1]], axis=0))
 
     def result(s):
         return zb[s * n:(s + 1) * n, 0:n], zb[s * n:(s + 1) * n, n:2 * n]
@@ -366,15 +368,6 @@
         wait_send(phase)
 
 
-def move(src, dst, sem):
-    pieces = [(i, j) for i in range(src.shape[0]) for j in range(src.shape[1])]
-    copies = [pltpu.make_async_copy(src.at[i, j], dst.at[i, j], sem.at[i, j]) for i, j in pieces]
-    for copy in copies:
-        copy.start()
-    for copy in copies:
-        copy.wait()
-
-
 def local(nr, nc, object_field, probe_field, intensity, counts, offsets):
     n = object_field.shape[-1]
     b = BORDER
@@ -390,7 +383,7 @@
         pltpu.VMEM((phases, 2, n // 2, n), F32),
         pltpu.VMEM((phases, 4, b // 2, n), F32),
     ]
-    updated = pl.pallas_call(
+    return pl.pallas_call(
         functools.partial(kernel, nr, nc),
         out_shape=jax.ShapeDtypeStruct(object_field.shape, F32),
         in_specs=[hbm, hbm, hbm, smem, smem, hbm],
@@ -420,14 +413,6 @@
             collective_id=0, has_side_effects=True, vmem_limit_bytes=63 * 1024 * 1024),
     )(object_field, probe_field, intensity, counts, jnp.swapaxes(offsets[0, 0], 0, 1),
       jnp.asarray(tabs))
-    return pl.pallas_call(
-        move,
-        out_shape=jax.ShapeDtypeStruct(updated.shape, F32),
-        in_specs=[hbm],
-        out_specs=hbm,
-        scratch_shapes=[pltpu.SemaphoreType.DMA(updated.shape[:2])],
-        compiler_params=pltpu.CompilerParams(vmem_limit_bytes=63 * 1024 * 1024),
-    )(updated)
 
 
 def solution(mesh):

time: 41.4 us -> 34 us (0.82)
  Pallas kernels: 40.5 us -> 31.5 us
  local copies, waits for them, and re-layouts: 0 us -> 1.67 us
    pallas_call x1 -> x0, Pallas kernels: 9.08 us -> none  [local(): pl.pallas_call(move, out_shape=jax.ShapeDtypeStruct(updated.shape, F32),...]
    unnamed x0 -> x1, local copies, waits for them, and re-layouts: none -> 1.67 us
where the time goes in v4:
time: 34 us; the launch traced here: 33.8 us
  Pallas kernels  31.5 us (93%)
  local copies, waits for them, and re-layouts  1.67 us (5%)
  between operations  0.66 us (2%)
    pallas_call x1, Pallas kernels, local(): pl.pallas_call(functools.partial(kernel, nr, nc), out_shape=jax.ShapeDtyp...  31.5 us
    unnamed x1, local copies, waits for them, and re-layouts  1.67 us

profile of v4, /device:TPU:1, one launch (start us, length us, event | category | flops | bytes accessed | tf_op | source)
XLA Modules:
  0.0 33.8 jit_solution(18356666969419828946)
XLA Ops:
  0.7 31.5 %shard_map.64 = f32[2,2,128,128]{3,2,1,0:T(8,128)} custom-call(f32[2,2,128,128]{3,2,1,0:T(8,128)} %obj_h.1, f32[2,128,128]{2,1,0:T(8,128)} %probe_h.1, f32[1,1,6,128,128]{4,3,2,1,0:T(8,128)} %inten_h.1, s32[1,1]{1,0:T(1,128)S(6)} %copy.8.counts, s32[2,6]{1,0:T(2,128)} %bitcast.3, bf16[4,2,256,256]{3,2,1,0:T(8,128)(2,1)} %constant.2.clone.tabs_h), custom_call_target="tpu_custom_call" | custom-call | tf_op jit(solution)/shard_map/pallas_call | solution.py:386
  32.1 1.7 %copy.9 = f32[2,2,128,128]{3,2,1,0:T(8,128)} copy(f32[2,2,128,128]{3,2,1,0:T(8,128)} %shard_map.64) | data formatting | bytes 524288
